TPU v7x, 32 devices: a whole 2x2x4 slice. The times are simulated.
32 devices in a mesh: section: 4 (over z), ctx: 4 (over x, core), dp: 2 (over y).
Axes of the slice: x: 2, y: 2, z: 4, core: 2. Of those that a mesh axis runs over, the one named last changes fastest.
Arguments:
- stream: bfloat16 [4, 256, 8192], P('section', 'dp', 'ctx'), may hold values from -6 to 6
- norm_gain: float32 [4, 8192], P('section', 'ctx'), may hold values from 0.5 to 2
- w_router: bfloat16 [4, 8192], P('section', 'ctx'), may hold values from -0.0625 to 0.0625
- w_gate: bfloat16 [4, 8192, 14336], P('section', 'ctx', 'dp'), may hold values from -0.0625 to 0.0625
- w_up: bfloat16 [4, 8192, 14336], P('section', 'ctx', 'dp'), may hold values from -0.0625 to 0.0625
- w_down: bfloat16 [4, 14336, 8192], P('section', 'dp', 'ctx'), may hold values from -0.046875 to 0.046875
- keep_rows: int32 [2, 4, 2, 32], P(None, 'section', 'dp'), may hold values from -1 to 127, as said below
Outputs:
- advanced: bfloat16 [4, 256, 8192], P('section', 'dp', 'ctx')
Inputs may be any that keep to these rules, and one draw needn't show every extreme that they name: `keep_rows`: each list holds distinct row indices first, then -1 in its empty slots. Over the 2 lists of one tick and section exactly 32 rows are kept; in each tick and section some list is full and some is empty.
All inputs are finite; a program needn't handle non-finite values.
Results may differ from a plain program's by a relative error of at most 0.005.
Values may be sent and summed in bfloat16 or wider, within the bound.
A program may use at most 192 MiB of HBM per device.

v0:
```python
import jax
import jax.numpy as jnp
from jax import lax
from jax.sharding import PartitionSpec as P

D = 8192
eps = 1e-05


def from_behind(value, axis, steps):
    count = lax.axis_size(axis)
    pairs = [(source, (source + steps) % count) for source in range(count)]
    return lax.ppermute(value, axis, pairs)


def hidden_block(normed, w_gate, w_up, w_down):
    row_piece = lax.all_gather(normed, "dp", axis=0, tiled=True)
    gate_part = jnp.dot(row_piece, w_gate, preferred_element_type=jnp.float32)
    up_part = jnp.dot(row_piece, w_up, preferred_element_type=jnp.float32)
    partial_value = jnp.stack([gate_part, up_part], axis=1)
    summed = lax.psum(partial_value, "ctx")
    hidden = (jax.nn.silu(summed[:, 0]) * summed[:, 1]).astype(jnp.bfloat16)
    return lax.psum_scatter(
        jnp.dot(hidden, w_down, preferred_element_type=jnp.float32).astype(jnp.bfloat16),
        "dp",
        scatter_dimension=0,
        tiled=True,
    ).astype(jnp.float32)


def routed_layer(stream, keep_list, gain_row, router, w_gate, w_up, w_down):
    is_kept = keep_list >= 0
    picked = jnp.take(stream, jnp.maximum(keep_list, 0), axis=0)
    rows_wide = picked.astype(jnp.float32)
    squares = jnp.sum(rows_wide * rows_wide, axis=1)
    logits = jnp.sum(rows_wide * router.astype(jnp.float32)[None, :], axis=1)
    squares, logits = lax.psum((squares, logits), "ctx")
    scaling = lax.rsqrt(squares / D + eps)
    normed = jnp.where(
        is_kept[:, None], rows_wide * scaling[:, None] * gain_row[None, :], 0.0
    ).astype(jnp.bfloat16)
    update = hidden_block(normed, w_gate, w_up, w_down)
    new_rows = (rows_wide + jax.nn.sigmoid(logits)[:, None] * update).astype(jnp.bfloat16)
    target = jnp.where(is_kept, keep_list, stream.shape[0])
    return stream.at[target].set(new_rows, mode="drop")


def local(stream, norm_gain, w_router, w_gate, w_up, w_down, keep_rows):
    first_pass = routed_layer(
        stream[0], keep_rows[0, 0, 0], norm_gain[0], w_router[0], w_gate[0], w_up[0], w_down[0]
    )
    passed = from_behind(first_pass, "section", 1)
    second_pass = routed_layer(
        passed, keep_rows[1, 0, 0], norm_gain[0], w_router[0], w_gate[0], w_up[0], w_down[0]
    )
    section_place = lax.axis_index("section")
    result = jnp.where(section_place == 0, passed, second_pass)
    return result[None]


def solution(mesh):
    return jax.shard_map(
        local,
        mesh=mesh,
        in_specs=(
            P("section", "dp", "ctx"),
            P("section", "ctx"),
            P("section", "ctx"),
            P("section", "ctx", "dp"),
            P("section", "ctx", "dp"),
            P("section", "dp", "ctx"),
            P(None, "section", "dp", None),
        ),
        out_specs=P("section", "dp", "ctx"),
        check_vma=False,
    )
```

profile of v0, /device:TPU:0, one launch (start us, length us, event | category | flops | bytes accessed | tf_op | source)
XLA Modules:
  0.0 325.9 jit_solution(13672440571319732338)
XLA Ops:
  6.5 0.0 all-reduce.5.cloned.1.call-start
  6.5 1.0 copy.13
  7.6 0.7 compare_and_fusion
  8.3 0.7 compare_bitcast_fusion
  8.9 0.7 mul.113
  9.7 0.7 gather_fusion
  10.3 0.2 fusion.36
  10.5 8.3 %all-reduce.1 = (f32[32]{0:T(128)S(1)}, f32[32]{0:T(128)S(1)}) all-reduce(f32[32]{0:T(128)S(1)} %get-tuple-element.9, f32[32]{0:T(128)S(1)} %get-tuple-element.8), channel_id=1, replica_groups=mesh['section'=4,'ctx'=4,'dp'=2] {'ctx'}, use_global_device_ids=true, to_apply=%region_3.5 | all-reduce | flops 64 | bytes 512 | tf_op jit(solution)/shard_map/psum | solution.py:37
  18.9 0.8 fusion.40
  19.7 5.6 %all_gather.6 = bf16[64,2048]{1,0:T(8,128)(2,1)S(1)} all-gather(bf16[32,2048]{1,0:T(8,128)(2,1)S(1)} %fusion.40), channel_id=1, replica_groups=mesh['section'=4,'ctx'=4,'dp'=2] {'dp'}, dimensions={0}, use_global_device_ids=true | all-gather | bytes 393216 | tf_op jit(solution)/shard_map/all_gather | solution.py:17
  25.4 12.0 %fusion.12 = f32[64,1,7168]{2,0,1:T(8,128)S(1)} fusion(bf16[64,2048]{1,0:T(8,128)(2,1)S(1)} %all_gather.6, bf16[1,2048,7168]{2,1,0:T(8,128)(2,1)} %param.12), kind=kOutput, calls=%fused_computation.16 | convolution fusion | flops 1879048192 | bytes 31457280 | tf_op jit(solution)/shard_map/dot_general | solution.py:18
  37.3 12.0 %fusion.18 = f32[64,1,7168]{2,0,1:T(8,128)S(1)} fusion(bf16[64,2048]{1,0:T(8,128)(2,1)S(1)} %all_gather.6, bf16[1,2048,7168]{2,1,0:T(8,128)(2,1)} %param.13), kind=kOutput, calls=%fused_computation.18 | convolution fusion | flops 1879048192 | bytes 31457280 | tf_op jit(solution)/shard_map/dot_general | solution.py:19
  49.3 2.1 pad_maximum_fusion
  51.4 0.0 all-reduce.5.cloned.1.call-update
  51.5 0.0 copy-start.1
  51.5 0.0 copy-start
  51.5 0.0 reduce-scatter.3.cloned.1.call-start
  51.5 77.4 %all-reduce.5.cloned.1.call-done = f32[64,2,7168]{2,0,1:T(8,128)} async-done(((f32[64,2,7168]{2,0,1:T(8,128)}), f32[64,2,7168]{2,0,1:T(8,128)}) %all-reduce.5.cloned.1.call-update) | async-done | bytes 3670032 | tf_op jit(solution)/shard_map/psum | solution.py:21
  128.9 16.4 %fusion.24 = bf16[64,2048]{1,0:T(8,128)(2,1)} fusion(bf16[1,7168,2048]{2,1,0:T(8,128)(2,1)} %param.14, f32[64,2,7168]{2,0,1:T(8,128)} %all-reduce.5.cloned.1.call-done), kind=kOutput, calls=%fused_computation.22 | convolution fusion | flops 1881931776 | bytes 33292288 | tf_op jit(solution)/shard_map/dot_general | solution.py:24
  145.3 0.0 reduce-scatter.3.cloned.1.call-update
  145.3 0.0 all-reduce.7.cloned.1.call-start
  145.4 0.0 copy-done.1
  145.4 11.9 %reduce-scatter.3.cloned.1.call-done = bf16[32,2048]{1,0:T(8,128)(2,1)} async-done(((bf16[64,2048]{1,0:T(8,128)(2,1)}), bf16[32,2048]{1,0:T(8,128)(2,1)}) %reduce-scatter.3.cloned.1.call-update) | async-done | bytes 131088 | tf_op jit(solution)/shard_map/reduce_scatter | solution.py:23
  157.3 1.6 scatter_custom_fusion
  158.9 1.5 collective-permute-start
  160.4 14.0 %collective-permute-done = bf16[128,2048]{1,0:T(8,128)(2,1)S(1)} collective-permute-done((bf16[128,2048]{1,0:T(8,128)(2,1)S(1)}, bf16[128,2048]{1,0:T(8,128)(2,1)S(1)}, u32[]{:S(2)}, u32[]{:S(2)}) %collective-permute-start) | collective-permute-done | bytes 524320 | tf_op jit(solution)/shard_map/ppermute | solution.py:13
  174.4 0.6 gather_fusion.1
  175.0 0.2 fusion.42
  175.3 5.7 %all-reduce = (f32[32]{0:T(128)S(1)}, f32[32]{0:T(128)S(1)}) all-reduce(f32[32]{0:T(128)S(1)} %get-tuple-element.7, f32[32]{0:T(128)S(1)} %get-tuple-element.6), channel_id=1, replica_groups=mesh['section'=4,'ctx'=4,'dp'=2] {'ctx'}, use_global_device_ids=true, to_apply=%region_10.12 | all-reduce | flops 64 | bytes 512 | tf_op jit(solution)/shard_map/psum | solution.py:37
  181.0 0.0 copy-done
  181.0 0.1 fusion.46
  181.1 6.1 %all_gather.7 = bf16[64,2048]{1,0:T(8,128)(2,1)S(1)} all-gather(bf16[32,2048]{1,0:T(8,128)(2,1)S(1)} %fusion.46), channel_id=1, replica_groups=mesh['section'=4,'ctx'=4,'dp'=2] {'dp'}, dimensions={0}, use_global_device_ids=true | all-gather | bytes 393216 | tf_op jit(solution)/shard_map/all_gather | solution.py:17
  187.2 12.0 %fusion.15 = f32[64,1,7168]{2,0,1:T(8,128)S(1)} fusion(bf16[64,2048]{1,0:T(8,128)(2,1)S(1)} %all_gather.7, bf16[1,2048,7168]{2,1,0:T(8,128)(2,1)} %param.12), kind=kOutput, calls=%fused_computation.17 | convolution fusion | flops 1879048192 | bytes 31457280 | tf_op jit(solution)/shard_map/dot_general | solution.py:18
  199.2 12.0 %fusion.21 = f32[64,1,7168]{2,0,1:T(8,128)S(1)} fusion(bf16[64,2048]{1,0:T(8,128)(2,1)S(1)} %all_gather.7, bf16[1,2048,7168]{2,1,0:T(8,128)(2,1)} %param.13), kind=kOutput, calls=%fused_computation.19 | convolution fusion | flops 1879048192 | bytes 31457280 | tf_op jit(solution)/shard_map/dot_general | solution.py:19
  211.2 2.1 pad_maximum_fusion.1
  213.3 0.0 all-reduce.7.cloned.1.call-update
  213.3 0.0 reduce-scatter.5.cloned.1.call-start
  213.4 75.2 %all-reduce.7.cloned.1.call-done = f32[64,2,7168]{2,0,1:T(8,128)} async-done(((f32[64,2,7168]{2,0,1:T(8,128)}), f32[64,2,7168]{2,0,1:T(8,128)}) %all-reduce.7.cloned.1.call-update) | async-done | bytes 3670032 | tf_op jit(solution)/shard_map/psum | solution.py:21
  288.6 16.4 %fusion.27 = bf16[64,2048]{1,0:T(8,128)(2,1)} fusion(bf16[1,7168,2048]{2,1,0:T(8,128)(2,1)} %param.14, f32[64,2,7168]{2,0,1:T(8,128)} %all-reduce.7.cloned.1.call-done), kind=kOutput, calls=%fused_computation.23 | convolution fusion | flops 1881931776 | bytes 33292288 | tf_op jit(solution)/shard_map/dot_general | solution.py:24
  305.0 0.0 reduce-scatter.5.cloned.1.call-update
  305.1 11.9 %reduce-scatter.5.cloned.1.call-done = bf16[32,2048]{1,0:T(8,128)(2,1)} async-done(((bf16[64,2048]{1,0:T(8,128)(2,1)}), bf16[32,2048]{1,0:T(8,128)(2,1)}) %reduce-scatter.5.cloned.1.call-update) | async-done | bytes 131088 | tf_op jit(solution)/shard_map/reduce_scatter | solution.py:23
  316.9 1.6 scatter_custom_fusion.1
  318.5 0.9 select_bitcast_fusion
  (8 shorter events, 0.1 us)
Async XLA Ops:
  6.5 122.4 %all-reduce.5.cloned.1.call-start = ((), (), s32[]{:S(2)}) async-start(), calls=%async_computation.2 | async-start | bytes 7340032 | tf_op jit(solution)/shard_map/psum | solution.py:21
  51.5 93.9 %copy-start.1 = (s32[2,1,1,32]{3,2,1,0:T(1,128)S(1)}, s32[2,1,1,32]{3,2,1,0:T(1,128)}, u32[]{:S(2)}) copy-start(s32[2,1,1,32]{3,2,1,0:T(1,128)} %param.15) | copy-start | bytes 772
  51.5 129.5 %copy-start = (f32[1,2048]{1,0:T(1,128)S(1)}, f32[1,2048]{1,0:T(1,128)}, u32[]{:S(2)}) copy-start(f32[1,2048]{1,0:T(1,128)} %param.10) | copy-start | bytes 24580
  51.5 105.8 %reduce-scatter.3.cloned.1.call-start = ((), (), s32[]{:S(2)}) async-start(), calls=%async_computation.3 | async-start | bytes 393216 | tf_op jit(solution)/shard_map/reduce_scatter | solution.py:23
  145.3 143.3 %all-reduce.7.cloned.1.call-start = ((), (), s32[]{:S(2)}) async-start(), calls=%async_computation.4 | async-start | bytes 7340032 | tf_op jit(solution)/shard_map/psum | solution.py:21
  158.9 15.5 %collective-permute-start = (bf16[128,2048]{1,0:T(8,128)(2,1)S(1)}, bf16[128,2048]{1,0:T(8,128)(2,1)S(1)}, u32[]{:S(2)}, u32[]{:S(2)}) collective-permute-start(bf16[128,2048]{1,0:T(8,128)(2,1)S(1)} %scatter_custom_fusion), channel_id=1, source_target_pairs={{0,8},{8,16},{16,24},{24,0},{1,9},{9,17},{17,25},{25,1},{2,10},{10... | collective-permute-start | bytes 1572872 | tf_op jit(solution)/shard_map/ppermute | solution.py:13
  213.3 103.6 %reduce-scatter.5.cloned.1.call-start = ((), (), s32[]{:S(2)}) async-start(), calls=%async_computation.5 | async-start | bytes 393216 | tf_op jit(solution)/shard_map/reduce_scatter | solution.py:23
Sparse Core Ops, SparseCore 0:
  51.6 77.3 all-reduce.4
  145.5 11.7 reduce-scatter.2
  213.4 75.1 all-reduce.6
  305.1 11.7 reduce-scatter.4
where the time goes:
time: 326 us
  waiting for transfers between devices  190 us (58%)
  matrix products  80.7 us (25%)
  blocking collectives  25.8 us (8%)
  between operations  13.3 us (4%)
  other arithmetic  11.7 us (4%)
    psum x2, waiting for transfers between devices, hidden_block(): summed = lax.psum(partial_value, 'ctx')  153 us
    dot_general x2, matrix products, hidden_block(): jnp.dot(hidden, w_down, preferred_element_type=jnp.float32)  32.8 us
    dot_general x2, matrix products, hidden_block(): up_part = jnp.dot(row_piece, w_up, preferred_element_type=jnp.float32)  24 us
    dot_general x2, matrix products, hidden_block(): gate_part = jnp.dot(row_piece, w_gate, preferred_element_type=jnp.float32)  24 us
    reduce_scatter x2, waiting for transfers between devices, hidden_block(): lax.psum_scatter(jnp.dot(hidden, w_down, preferred_element_type=jnp.float...  23.7 us
    psum x2, blocking collectives, routed_layer(): squares, logits = lax.psum((squares, logits), 'ctx')  14 us
    ppermute x1, waiting for transfers between devices, from_behind(): return lax.ppermute(value, axis, pairs)  14 us
    all_gather x2, blocking collectives, hidden_block(): row_piece = lax.all_gather(normed, 'dp', axis=0, tiled=True)  11.7 us
  transfers between devices with their start and end apart: 5, of which 5 were waited for; matrix products, arithmetic and copies ran while one was open for 0% of the time, Pallas kernels for 0%

commit v1 on v0

--- a/solution.py
+++ b/solution.py
@@ -18,7 +18,7 @@
     gate_part = jnp.dot(row_piece, w_gate, preferred_element_type=jnp.float32)
     up_part = jnp.dot(row_piece, w_up, preferred_element_type=jnp.float32)
     partial_value = jnp.stack([gate_part, up_part], axis=1)
-    summed = lax.psum(partial_value, "ctx")
+    summed = jnp.sum(lax.all_gather(partial_value, "ctx"), axis=0)
     hidden = (jax.nn.silu(summed[:, 0]) * summed[:, 1]).astype(jnp.bfloat16)
     return lax.psum_scatter(
         jnp.dot(hidden, w_down, preferred_element_type=jnp.float32).astype(jnp.bfloat16),

time: 326 us -> 377 us (1.16)
  waiting for transfers between devices: 190 us -> 224 us
  other arithmetic: 11.7 us -> 28.4 us
    all_gather x0 -> x2, waiting for transfers between devices: none -> 187 us  [hidden_block(): summed = jnp.sum(lax.all_gather(partial_value, 'ctx'), axis=0)]
    psum x2 -> x0, waiting for transfers between devices: 153 us -> none  [hidden_block(): summed = lax.psum(partial_value, 'ctx')]
    reduce_sum x0 -> x2, other arithmetic: none -> 16.9 us  [hidden_block(): summed = jnp.sum(lax.all_gather(partial_value, 'ctx'), axis=0)]
where the time goes in v1:
time: 377 us
  waiting for transfers between devices  224 us (59%)
  matrix products  80.8 us (21%)
  other arithmetic  28.4 us (8%)
  blocking collectives  25.8 us (7%)
  between operations  13.3 us (4%)
    all_gather x2, waiting for transfers between devices, hidden_block(): summed = jnp.sum(lax.all_gather(partial_value, 'ctx'), axis=0)  187 us
    dot_general x2, matrix products, hidden_block(): jnp.dot(hidden, w_down, preferred_element_type=jnp.float32)  32.8 us
    dot_general x2, matrix products, hidden_block(): up_part = jnp.dot(row_piece, w_up, preferred_element_type=jnp.float32)  24 us
    dot_general x2, matrix products, hidden_block(): gate_part = jnp.dot(row_piece, w_gate, preferred_element_type=jnp.float32)  24 us
    reduce_scatter x2, waiting for transfers between devices, hidden_block(): lax.psum_scatter(jnp.dot(hidden, w_down, preferred_element_type=jnp.float...  23.5 us
    reduce_sum x2, other arithmetic, hidden_block(): summed = jnp.sum(lax.all_gather(partial_value, 'ctx'), axis=0)  16.9 us
    psum x2, blocking collectives, routed_layer(): squares, logits = lax.psum((squares, logits), 'ctx')  14 us
    ppermute x1, waiting for transfers between devices, from_behind(): return lax.ppermute(value, axis, pairs)  14 us
  transfers between devices with their start and end apart: 5, of which 5 were waited for; matrix products, arithmetic and copies ran while one was open for 0% of the time, Pallas kernels for 0%

profile of v1, /device:TPU:0, one launch (start us, length us, event | category | flops | bytes accessed | tf_op | source)
XLA Modules:
  0.0 376.6 jit_solution(18255667798704496331)
XLA Ops:
  6.5 0.0 all-gather.5.cloned.1.call-start
  6.5 1.0 copy.11
  7.6 0.7 compare_and_fusion
  8.3 0.7 compare_bitcast_fusion
  8.9 0.7 mul.113
  9.7 0.7 gather_fusion
  10.3 0.2 fusion.36
  10.5 8.3 %all-reduce.1 = (f32[32]{0:T(128)S(1)}, f32[32]{0:T(128)S(1)}) all-reduce(f32[32]{0:T(128)S(1)} %get-tuple-element.9, f32[32]{0:T(128)S(1)} %get-tuple-element.8), channel_id=1, replica_groups=mesh['section'=4,'ctx'=4,'dp'=2] {'ctx'}, use_global_device_ids=true, to_apply=%region_3.5 | all-reduce | flops 64 | bytes 512 | tf_op jit(solution)/shard_map/psum | solution.py:37
  18.9 0.8 fusion.40
  19.7 5.6 %all_gather.18 = bf16[64,2048]{1,0:T(8,128)(2,1)S(1)} all-gather(bf16[32,2048]{1,0:T(8,128)(2,1)S(1)} %fusion.40), channel_id=1, replica_groups=mesh['section'=4,'ctx'=4,'dp'=2] {'dp'}, dimensions={0}, use_global_device_ids=true | all-gather | bytes 393216 | tf_op jit(solution)/shard_map/all_gather | solution.py:17
  25.4 12.0 %fusion.12 = f32[64,1,7168]{2,0,1:T(8,128)S(1)} fusion(bf16[64,2048]{1,0:T(8,128)(2,1)S(1)} %all_gather.18, bf16[1,2048,7168]{2,1,0:T(8,128)(2,1)} %param.12), kind=kOutput, calls=%fused_computation.16 | convolution fusion | flops 1879048192 | bytes 31457280 | tf_op jit(solution)/shard_map/dot_general | solution.py:18
  37.3 12.0 %fusion.18 = f32[64,1,7168]{2,0,1:T(8,128)S(1)} fusion(bf16[64,2048]{1,0:T(8,128)(2,1)S(1)} %all_gather.18, bf16[1,2048,7168]{2,1,0:T(8,128)(2,1)} %param.13), kind=kOutput, calls=%fused_computation.18 | convolution fusion | flops 1879048192 | bytes 31457280 | tf_op jit(solution)/shard_map/dot_general | solution.py:19
  49.3 2.0 pad_maximum_fusion
  51.4 0.0 all-gather.5.cloned.1.call-update
  51.4 0.0 reduce-scatter.3.cloned.1.call-start
  51.5 94.5 %all-gather.5.cloned.1.call-done = f32[256,2,7168]{2,0,1:T(8,128)} async-done(((f32[64,2,7168]{2,0,1:T(8,128)}), f32[256,2,7168]{2,0,1:T(8,128)}) %all-gather.5.cloned.1.call-update) | async-done | bytes 14680080 | tf_op jit(solution)/shard_map/all_gather | solution.py:21
  145.9 8.4 %reduce_sum.56 = f32[64,2,7168]{2,0,1:T(8,128)} reduce(f32[4,64,2,7168]{3,1,0,2:T(8,128)} %bitcast.71, f32[]{:T(128)} %constant.13.clone.1), dimensions={0}, to_apply=%region_4.6 | reduce | flops 2752512 | bytes 18350084 | tf_op jit(solution)/shard_map/reduce_sum | solution.py:21
  154.4 0.0 copy-start.1
  154.4 0.0 copy-start
  154.4 16.4 %fusion.24 = bf16[64,2048]{1,0:T(8,128)(2,1)} fusion(bf16[1,7168,2048]{2,1,0:T(8,128)(2,1)} %param.14, f32[64,2,7168]{2,0,1:T(8,128)} %reduce_sum.56), kind=kOutput, calls=%fused_computation.22 | convolution fusion | flops 1881931776 | bytes 33292288 | tf_op jit(solution)/shard_map/dot_general | solution.py:24
  170.8 0.0 reduce-scatter.3.cloned.1.call-update
  170.8 0.0 all-gather.7.cloned.1.call-start
  170.9 0.0 copy-done.1
  170.9 11.8 %reduce-scatter.3.cloned.1.call-done = bf16[32,2048]{1,0:T(8,128)(2,1)} async-done(((bf16[64,2048]{1,0:T(8,128)(2,1)}), bf16[32,2048]{1,0:T(8,128)(2,1)}) %reduce-scatter.3.cloned.1.call-update) | async-done | bytes 131088 | tf_op jit(solution)/shard_map/reduce_scatter | solution.py:23
  182.6 1.6 scatter_custom_fusion
  184.2 1.5 collective-permute-start
  185.7 14.0 %collective-permute-done = bf16[128,2048]{1,0:T(8,128)(2,1)S(1)} collective-permute-done((bf16[128,2048]{1,0:T(8,128)(2,1)S(1)}, bf16[128,2048]{1,0:T(8,128)(2,1)S(1)}, u32[]{:S(2)}, u32[]{:S(2)}) %collective-permute-start) | collective-permute-done | bytes 524320 | tf_op jit(solution)/shard_map/ppermute | solution.py:13
  199.7 0.6 gather_fusion.1
  200.4 0.2 fusion.42
  200.6 5.7 %all-reduce = (f32[32]{0:T(128)S(1)}, f32[32]{0:T(128)S(1)}) all-reduce(f32[32]{0:T(128)S(1)} %get-tuple-element.7, f32[32]{0:T(128)S(1)} %get-tuple-element.6), channel_id=1, replica_groups=mesh['section'=4,'ctx'=4,'dp'=2] {'ctx'}, use_global_device_ids=true, to_apply=%region_10.12 | all-reduce | flops 64 | bytes 512 | tf_op jit(solution)/shard_map/psum | solution.py:37
  206.3 0.0 copy-done
  206.3 0.1 fusion.46
  206.4 6.1 %all_gather.21 = bf16[64,2048]{1,0:T(8,128)(2,1)S(1)} all-gather(bf16[32,2048]{1,0:T(8,128)(2,1)S(1)} %fusion.46), channel_id=1, replica_groups=mesh['section'=4,'ctx'=4,'dp'=2] {'dp'}, dimensions={0}, use_global_device_ids=true | all-gather | bytes 393216 | tf_op jit(solution)/shard_map/all_gather | solution.py:17
  212.5 12.0 %fusion.15 = f32[64,1,7168]{2,0,1:T(8,128)S(1)} fusion(bf16[64,2048]{1,0:T(8,128)(2,1)S(1)} %all_gather.21, bf16[1,2048,7168]{2,1,0:T(8,128)(2,1)} %param.12), kind=kOutput, calls=%fused_computation.17 | convolution fusion | flops 1879048192 | bytes 31457280 | tf_op jit(solution)/shard_map/dot_general | solution.py:18
  224.5 12.0 %fusion.21 = f32[64,1,7168]{2,0,1:T(8,128)S(1)} fusion(bf16[64,2048]{1,0:T(8,128)(2,1)S(1)} %all_gather.21, bf16[1,2048,7168]{2,1,0:T(8,128)(2,1)} %param.13), kind=kOutput, calls=%fused_computation.19 | convolution fusion | flops 1879048192 | bytes 31457280 | tf_op jit(solution)/shard_map/dot_general | solution.py:19
  236.5 2.0 pad_maximum_fusion.1
  238.5 0.0 all-gather.7.cloned.1.call-update
  238.6 0.0 reduce-scatter.5.cloned.1.call-start
  238.6 92.3 %all-gather.7.cloned.1.call-done = f32[256,2,7168]{2,0,1:T(8,128)} async-done(((f32[64,2,7168]{2,0,1:T(8,128)}), f32[256,2,7168]{2,0,1:T(8,128)}) %all-gather.7.cloned.1.call-update) | async-done | bytes 14680080 | tf_op jit(solution)/shard_map/all_gather | solution.py:21
  331.0 8.4 %reduce_sum.59 = f32[64,2,7168]{2,0,1:T(8,128)} reduce(f32[4,64,2,7168]{3,1,0,2:T(8,128)} %bitcast.70, f32[]{:T(128)} %constant.13.clone.1), dimensions={0}, to_apply=%region_11.13 | reduce | flops 2752512 | bytes 18350084 | tf_op jit(solution)/shard_map/reduce_sum | solution.py:21
  339.4 16.4 %fusion.27 = bf16[64,2048]{1,0:T(8,128)(2,1)} fusion(bf16[1,7168,2048]{2,1,0:T(8,128)(2,1)} %param.14, f32[64,2,7168]{2,0,1:T(8,128)} %reduce_sum.59), kind=kOutput, calls=%fused_computation.23 | convolution fusion | flops 1881931776 | bytes 33292288 | tf_op jit(solution)/shard_map/dot_general | solution.py:24
  355.8 0.0 reduce-scatter.5.cloned.1.call-update
  355.9 11.8 %reduce-scatter.5.cloned.1.call-done = bf16[32,2048]{1,0:T(8,128)(2,1)} async-done(((bf16[64,2048]{1,0:T(8,128)(2,1)}), bf16[32,2048]{1,0:T(8,128)(2,1)}) %reduce-scatter.5.cloned.1.call-update) | async-done | bytes 131088 | tf_op jit(solution)/shard_map/reduce_scatter | solution.py:23
  367.6 1.6 scatter_custom_fusion.1
  369.2 0.9 select_bitcast_fusion
  (8 shorter events, 0.1 us)
Async XLA Ops:
  6.5 139.4 %all-gather.5.cloned.1.call-start = ((), (), s32[]{:S(2)}) async-start(), calls=%async_computation.4 | async-start | bytes 18350080 | tf_op jit(solution)/shard_map/all_gather | solution.py:21
  51.4 131.2 %reduce-scatter.3.cloned.1.call-start = ((), (), s32[]{:S(2)}) async-start(), calls=%async_computation.2 | async-start | bytes 393216 | tf_op jit(solution)/shard_map/reduce_scatter | solution.py:23
  154.4 16.5 %copy-start.1 = (s32[2,1,1,32]{3,2,1,0:T(1,128)S(1)}, s32[2,1,1,32]{3,2,1,0:T(1,128)}, u32[]{:S(2)}) copy-start(s32[2,1,1,32]{3,2,1,0:T(1,128)} %param.15) | copy-start | bytes 772
  154.4 51.9 %copy-start = (f32[1,2048]{1,0:T(1,128)S(1)}, f32[1,2048]{1,0:T(1,128)}, u32[]{:S(2)}) copy-start(f32[1,2048]{1,0:T(1,128)} %param.10) | copy-start | bytes 24580
  170.8 160.2 %all-gather.7.cloned.1.call-start = ((), (), s32[]{:S(2)}) async-start(), calls=%async_computation.5 | async-start | bytes 18350080 | tf_op jit(solution)/shard_map/all_gather | solution.py:21
  184.2 15.5 %collective-permute-start = (bf16[128,2048]{1,0:T(8,128)(2,1)S(1)}, bf16[128,2048]{1,0:T(8,128)(2,1)S(1)}, u32[]{:S(2)}, u32[]{:S(2)}) collective-permute-start(bf16[128,2048]{1,0:T(8,128)(2,1)S(1)} %scatter_custom_fusion), channel_id=1, source_target_pairs={{0,8},{8,16},{16,24},{24,0},{1,9},{9,17},{17,25},{25,1},{2,10},{10... | collective-permute-start | bytes 1572872 | tf_op jit(solution)/shard_map/ppermute | solution.py:13
  238.6 129.1 %reduce-scatter.5.cloned.1.call-start = ((), (), s32[]{:S(2)}) async-start(), calls=%async_computation.3 | async-start | bytes 393216 | tf_op jit(solution)/shard_map/reduce_scatter | solution.py:23
Sparse Core Ops, SparseCore 0:
  51.5 94.3 all-gather.4
  170.9 11.6 reduce-scatter.2
  238.7 92.2 all-gather.6
  355.9 11.6 reduce-scatter.4
